TPU v7x, 256 devices: a whole 4x4x8 slice. The times are simulated.
256 devices in a mesh: tp: 8 (over y, core), dp: 32 (over z, x).
Axes of the slice: x: 4, y: 4, z: 8, core: 2. Of those that a mesh axis runs over, the one named last changes fastest.
Arguments:
- queries: bfloat16 [64, 8, 4, 8192], P('dp', None, None, 'tp'), may hold values from -100 to 100
- new_keys: bfloat16 [64, 8, 4, 1024], P('dp', None, None, 'tp'), may hold values from -12 to 12
- new_values: bfloat16 [64, 8, 4, 1024], P('dp', None, None, 'tp'), may hold values from -6 to 6
- key_pool: bfloat16 [5120, 64, 1024], P('dp', None, 'tp'), may hold values from -6 to 6
- value_pool: bfloat16 [5120, 64, 1024], P('dp', None, 'tp'), may hold values from -6 to 6
- out_weight: bfloat16 [8192, 8192], P('tp', 'dp'), may hold values from -0.0625 to 0.0625
- mem_len: int32 [64], replicated, may hold values from 426 to 5120, as said below
- assign: int32 [64], replicated, may hold values from 0 to 63, as said below
- block_table: int32 [64, 80], replicated, may hold values from 0 to 5119, as said below
Outputs:
- layer_out: bfloat16 [2048, 8192], P('tp', 'dp')
- decode_keys: bfloat16 [64, 5120, 1024], P('dp', None, 'tp')
- decode_values: bfloat16 [64, 5120, 1024], P('dp', None, 'tp')
Inputs may be any that keep to these rules, and one draw needn't show every extreme that they name: `mem_len`: some prompt's memory is exactly 5120 tokens long. `assign`: A permutation of the prompts; the slots of index d of dp are 2 * d to 2 * d + 1. `block_table`: page id g lies on index g // 160 of dp, at local page g % 160. Every page id appears exactly once in the table. For every pair of indices d and e of dp, exactly 5 of the table entries of the prompts in the slots of d lie on e. Entries past a prompt's memory are valid ids whose contents are not used.
All inputs are finite; a program needn't handle non-finite values.
Results may differ from a plain program's by a relative error of at most 0.019.
Values may be sent and summed in bfloat16 or wider, within the bound.
A program may use at most 64 MiB of HBM per device.

v0:
```python
import math

import jax
import jax.numpy as jnp
from jax import lax
from jax.sharding import PartitionSpec as P

HD = 128
QPK = 8


def slot_attention(query, memory_keys, memory_values, fresh_keys, fresh_values, length):
    sample_count = query.shape[0]
    step_count = query.shape[1]
    memory_span = memory_keys.shape[0]
    kv_heads = memory_keys.shape[1] // HD
    score_scale = 1.0 / math.sqrt(HD)
    query_heads = query.reshape(sample_count, step_count, kv_heads, QPK, HD)
    key_heads = memory_keys.reshape(memory_span, kv_heads, HD)
    value_heads = memory_values.reshape(memory_span, kv_heads, HD)
    fresh_key_heads = fresh_keys.reshape(sample_count, step_count, kv_heads, HD)
    fresh_value_heads = fresh_values.reshape(sample_count, step_count, kv_heads, HD)
    fresh_scores = (
        jnp.einsum(
            "ashgd,auhd->ashgu", query_heads, fresh_key_heads, preferred_element_type=jnp.float32
        )
        * score_scale
    )
    causal = jnp.arange(step_count)[:, None] >= jnp.arange(step_count)[None, :]
    fresh_scores = jnp.where(causal[None, :, None, None, :], fresh_scores, -jnp.inf)
    memory_scores = (
        jnp.einsum("ashgd,khd->ashgk", query_heads, key_heads, preferred_element_type=jnp.float32)
        * score_scale
    )
    usable = jnp.arange(memory_span, dtype=jnp.int32) < length
    memory_scores = jnp.where(usable[None, None, None, None, :], memory_scores, -jnp.inf)
    row_max = jnp.maximum(jnp.max(memory_scores, axis=-1), jnp.max(fresh_scores, axis=-1))
    memory_weights = jnp.exp(memory_scores - row_max[..., None])
    fresh_weights = jnp.exp(fresh_scores - row_max[..., None])
    row_total = jnp.sum(memory_weights, axis=-1) + jnp.sum(fresh_weights, axis=-1)
    weighted = jnp.einsum(
        "ashgk,khd->ashgd",
        memory_weights.astype(jnp.bfloat16),
        value_heads,
        preferred_element_type=jnp.float32,
    )
    weighted = weighted + jnp.einsum(
        "ashgu,auhd->ashgd",
        fresh_weights.astype(jnp.bfloat16),
        fresh_value_heads,
        preferred_element_type=jnp.float32,
    )
    mixed = weighted / row_total[..., None]
    return mixed.reshape(sample_count * step_count, -1).astype(jnp.bfloat16)


def local(
    queries, new_keys, new_values, key_pool, value_pool, out_weight, mem_len, assign, block_table
):
    devices = lax.axis_size("dp")
    own_index = lax.axis_index("dp")
    pool_pages, page_size, features = key_pool.shape
    slots_here = queries.shape[0]
    page_count = block_table.shape[1]
    entry_count = slots_here * page_count
    capacity = entry_count // devices
    tables = jnp.take(block_table, assign, axis=0).reshape(devices, entry_count)
    lengths = jnp.take(mem_len, assign, axis=0)
    source = tables // pool_pages
    local_page = tables % pool_pages
    page_start = jnp.arange(page_count, dtype=jnp.int32) * page_size
    used = (page_start[None, None, :] < lengths.reshape(devices, slots_here)[:, :, None]).reshape(
        devices, entry_count
    )
    owners = jnp.arange(devices, dtype=jnp.int32)
    hit_table = (source[:, :, None] == owners[None, None, :]).astype(jnp.int32)
    used_flag = used.astype(jnp.int32)[:, :, None]
    hit_used = hit_table * used_flag
    hit_unused = hit_table * (1 - used_flag)
    earlier_used = jnp.cumsum(hit_used, axis=1) - hit_used
    earlier_unused = jnp.cumsum(hit_unused, axis=1) - hit_unused
    total_used = jnp.sum(hit_used, axis=1)
    rank_each = jnp.where(used[:, :, None], earlier_used, total_used[:, None, :] + earlier_unused)
    rank_order = jnp.sum(rank_each * hit_table, axis=2)
    is_mine = source == own_index
    selected = is_mine[:, :, None] & (
        rank_order[:, :, None] == jnp.arange(capacity, dtype=jnp.int32)[None, None, :]
    )
    send_index = jnp.sum(jnp.where(selected, local_page[:, :, None], 0), axis=1)
    send_keys = key_pool[send_index]
    send_values = value_pool[send_index]
    got_keys, got_values = (
        lax.all_to_all(send_keys, "dp", split_axis=0, concat_axis=0, tiled=True),
        lax.all_to_all(send_values, "dp", split_axis=0, concat_axis=0, tiled=True),
    )
    my_source = lax.dynamic_index_in_dim(source, own_index, 0, keepdims=False)
    my_order = lax.dynamic_index_in_dim(rank_order, own_index, 0, keepdims=False)
    where_from = my_source * capacity + my_order
    memory_span = page_count * page_size
    flat_keys = got_keys.reshape(devices * capacity, page_size, features)[where_from].reshape(
        slots_here, memory_span, features
    )
    flat_values = got_values.reshape(devices * capacity, page_size, features)[where_from].reshape(
        slots_here, memory_span, features
    )
    my_lengths = lax.dynamic_slice_in_dim(lengths, own_index * slots_here, slots_here)
    usable = jnp.arange(memory_span, dtype=jnp.int32)[None, :, None] < my_lengths[:, None, None]
    decode_keys = jnp.where(usable, flat_keys, jnp.zeros_like(flat_keys))
    decode_values = jnp.where(usable, flat_values, jnp.zeros_like(flat_values))
    slot_rows = []
    for slot_index in range(slots_here):
        slot_rows.append(
            slot_attention(
                queries[slot_index],
                decode_keys[slot_index],
                decode_values[slot_index],
                new_keys[slot_index],
                new_values[slot_index],
                my_lengths[slot_index],
            )
        )
    attention_rows = jnp.concatenate(slot_rows, axis=0)
    partial_out = jnp.dot(
        lax.all_gather(attention_rows, "dp", axis=0, tiled=True),
        out_weight,
        preferred_element_type=jnp.float32,
    )
    layer_out = lax.psum_scatter(
        partial_out.astype(jnp.bfloat16), "tp", scatter_dimension=0, tiled=True
    )
    return (layer_out, decode_keys, decode_values)


def solution(mesh):
    placed = (
        P("dp", None, None, "tp"),
        P("dp", None, None, "tp"),
        P("dp", None, None, "tp"),
        P("dp", None, "tp"),
        P("dp", None, "tp"),
        P("tp", "dp"),
        P(),
        P(),
        P(),
    )
    return jax.shard_map(
        local,
        mesh=mesh,
        in_specs=placed,
        out_specs=(P("tp", "dp"), P("dp", None, "tp"), P("dp", None, "tp")),
        check_vma=False,
    )
```

profile of v0, /device:TPU:4, one launch (start us, length us, event | category | flops | bytes accessed | tf_op | source)
XLA Modules:
  0.0 383.6 jit_solution(14409015781876058134)
XLA Ops:
  7.2 0.8 compare_select_fusion.2
  8.0 1.4 gather_fusion
  9.4 0.7 broadcast_select_fusion.1
  10.1 0.1 gather.27
  10.2 0.1 broadcast_in_dim.123
  10.3 0.1 broadcast_in_dim.124
  10.4 0.1 broadcast_in_dim.125
  10.5 1.4 gather_fusion.1
  11.9 0.1 gather.26
  12.1 0.1 lt.125
  12.2 0.1 lt.126
  12.2 0.1 lt.123
  12.4 0.6 select_reduce_fusion
  13.0 0.3 fusion.51
  13.3 1.2 pad_bitcast_fusion
  14.5 1.1 copy.50
  15.6 35.1 %reduce-window.14 = s32[32,32,2,128]{3,1,2,0:T(8,128)} reduce-window(s32[32,32,2,128]{3,1,2,0:T(8,128)} %bitcast.234, s32[]{:T(128)} %constant.47.clone.1), window={size=1x1x1x128 pad=0_0x0_0x0_0x127_0}, to_apply=%region_0.1 | reduce-window | flops 33292288 | bytes 2097156 | tf_op jit(solution)/shard_map/reduce-window
  50.7 2.5 slice.84
  53.2 1.7 copy.21
  54.9 0.1 fusion.63
  55.0 2.7 bitcast_bitcast_fusion.1
  57.7 1.1 copy.49
  58.8 35.3 %reduce-window.16 = s32[32,32,2,128]{3,1,2,0:T(8,128)} reduce-window(s32[32,32,2,128]{3,1,2,0:T(8,128)} %bitcast.235, s32[]{:T(128)} %constant.47.clone.1), window={size=1x1x1x128 pad=0_0x0_0x0_0x127_0}, to_apply=%region_3.4 | reduce-window | flops 33292288 | bytes 2097156 | tf_op jit(solution)/shard_map/reduce-window.2
  94.1 2.5 slice.87
  96.6 1.7 copy.25
  98.3 0.1 fusion.61
  98.4 1.6 bitcast_bitcast_fusion
  100.1 0.8 fusion.48
  100.8 0.2 select_reduce_fusion.1
  101.0 0.1 copy.28
  101.1 0.1 reshape.421
  101.3 2.5 gather_fusion.4
  103.8 11.6 %all-to-all-start.1 = ((bf16[32,5,64,128]{3,2,1,0:T(8,128)(2,1)}), bf16[32,5,64,128]{3,2,1,0:T(8,128)(2,1)}, u32[]{:S(2)}, u32[]{:S(2)}) async-start(bf16[32,5,64,128]{3,2,1,0:T(8,128)(2,1)} %bitcast.231), calls=%async_computation.1 | async-start | bytes 5242880 | tf_op jit(solution)/shard_map/all_to_all | solution.py:93
  115.4 4.3 %gather_fusion.2 = bf16[160,64,128]{2,1,0:T(8,128)(2,1)} fusion(bf16[160,64,128]{2,1,0:T(8,128)(2,1)} %param.13, s32[1024]{0:T(1024)S(1)} %pad_clamp_fusion.1), kind=kCustom, calls=%fused_computation.2 | custom fusion | bytes 5243520 | tf_op jit(solution)/shard_map/gather | solution.py:91
  119.7 56.3 %all-to-all-done.1 = bf16[32,5,64,128]{3,2,1,0:T(8,128)(2,1)} async-done(((bf16[32,5,64,128]{3,2,1,0:T(8,128)(2,1)}), bf16[32,5,64,128]{3,2,1,0:T(8,128)(2,1)}, u32[]{:S(2)}, u32[]{:S(2)}) %all-to-all-start.1) | async-done | bytes 2621472 | tf_op jit(solution)/shard_map/all_to_all | solution.py:93
  176.0 7.0 %all-to-all-start = ((bf16[32,5,64,128]{3,2,1,0:T(8,128)(2,1)}), bf16[32,5,64,128]{3,2,1,0:T(8,128)(2,1)}, u32[]{:S(2)}, u32[]{:S(2)}) async-start(bf16[32,5,64,128]{3,2,1,0:T(8,128)(2,1)} %bitcast.230), calls=%async_computation | async-start | bytes 5242880 | tf_op jit(solution)/shard_map/all_to_all | solution.py:94
  183.0 0.2 all-gather.2.cloned.1.call-start
  183.4 0.1 dynamic_slice.10
  183.5 0.6 fusion.78
  184.1 0.7 iota_compare_fusion.5
  184.7 0.7 iota_compare_fusion.4
  185.4 0.4 fusion.82
  185.8 0.4 fusion.80
  186.3 0.1 iota_compare_fusion.3
  186.4 4.3 %gather_fusion.5 = bf16[160,64,128]{2,1,0:T(8,128)(2,1)} fusion(bf16[160,64,128]{2,1,0:T(8,128)(2,1)} %bitcast.15, s32[1024]{0:T(1024)S(1)} %pad_clamp_fusion), kind=kCustom, calls=%fused_computation.5 | custom fusion | bytes 5243520 | tf_op jit(solution)/shard_map/gather | solution.py:100
  190.6 53.4 %all-to-all-done = bf16[32,5,64,128]{3,2,1,0:T(8,128)(2,1)} async-done(((bf16[32,5,64,128]{3,2,1,0:T(8,128)(2,1)}), bf16[32,5,64,128]{3,2,1,0:T(8,128)(2,1)}, u32[]{:S(2)}, u32[]{:S(2)}) %all-to-all-start) | async-done | bytes 2621472 | tf_op jit(solution)/shard_map/all_to_all | solution.py:94
  244.0 4.3 %gather_fusion.3 = bf16[160,64,128]{2,1,0:T(8,128)(2,1)} fusion(bf16[160,64,128]{2,1,0:T(8,128)(2,1)} %bitcast.6, s32[1024]{0:T(1024)S(1)} %pad_clamp_fusion), kind=kCustom, calls=%fused_computation.3 | custom fusion | bytes 5243520 | tf_op jit(solution)/shard_map/gather | solution.py:103
  248.3 6.1 %bitcast_select_fusion.1 = (bf16[2,5120,128]{2,1,0:T(8,128)(2,1)S(1)}, bf16[2,5120,128]{2,1,0:T(8,128)(2,1)S(1)}) fusion(pred[2,5120]{1,0:T(4,128)(4,1)S(1)} %iota_compare_fusion.3, bf16[2,5120,128]{2,1,0:T(8,128)(2,1)} %bitcast.233, bf16[2,5120,128]{2,1,0:T(8,128)(2,1)} %bitcast.232), kind=kLoop, calls=%fused_computation.25 | loop fusion | flops 2621440 | bytes 10496000 | tf_op jit(solution)/shard_map/jit(_where)/select_n | solution.py:109
  254.5 1.0 fusion.81
  255.5 0.1 fusion.53
  255.6 0.2 convolution_bitcast_fusion.1
  255.8 0.2 copy-done.4
  255.9 1.0 fusion.79
  257.0 0.1 fusion.55
  257.0 0.2 convolution_bitcast_fusion
  257.2 0.9 fusion.6
  258.1 0.9 fusion.36
  259.0 0.9 fusion.8
  259.9 0.9 fusion.39
  260.9 0.7 pad_maximum_fusion
  261.5 0.0 reduce-scatter.2.cloned.1.call-start
  261.6 77.2 %all-gather.2.cloned.1.call-done = bf16[2048,1024]{1,0:T(8,128)(2,1)} async-done(((bf16[64,1024]{1,0:T(8,128)(2,1)}), bf16[2048,1024]{1,0:T(8,128)(2,1)}) %all-gather.2.cloned.1.call-update) | async-done | bytes 4194320 | tf_op jit(solution)/shard_map/all_gather | solution.py:124
  338.8 4.4 %convolution_convert_fusion = bf16[2048,256]{1,0:T(8,128)(2,1)} fusion(bf16[2048,1024]{1,0:T(8,128)(2,1)} %all-gather.2.cloned.1.call-done, bf16[1024,256]{1,0:T(8,128)(2,1)S(1)} %copy-done.7), kind=kOutput, calls=%fused_computation.28 | convolution fusion | flops 1074266112 | bytes 5767168 | tf_op jit(solution)/shard_map/dot_general | solution.py:123
  343.3 33.4 %reduce-scatter.2.cloned.1.call-done = bf16[256,256]{1,0:T(8,128)(2,1)} async-done(((bf16[2048,256]{1,0:T(8,128)(2,1)}), bf16[256,256]{1,0:T(8,128)(2,1)}) %reduce-scatter.2.cloned.1.call-update) | async-done | bytes 131088 | tf_op jit(solution)/shard_map/reduce_scatter | solution.py:128
  (45 shorter events, 0.4 us)
Async XLA Ops:
  7.2 94.1 %copy-start = (bf16[160,64,128]{2,1,0:T(8,128)(2,1)S(1)}, bf16[160,64,128]{2,1,0:T(8,128)(2,1)}, u32[]{:S(2)}) copy-start(bf16[160,64,128]{2,1,0:T(8,128)(2,1)} %param.12) | copy-start | bytes 7864324
  54.9 2.8 copy-start.2
  98.3 1.8 copy-start.1
  103.8 72.2 %all-to-all-start.1 = ((bf16[32,5,64,128]{3,2,1,0:T(8,128)(2,1)}), bf16[32,5,64,128]{3,2,1,0:T(8,128)(2,1)}, u32[]{:S(2)}, u32[]{:S(2)}) async-start(bf16[32,5,64,128]{3,2,1,0:T(8,128)(2,1)} %bitcast.231), calls=%async_computation.1 | async-start | bytes 5242880 | tf_op jit(solution)/shard_map/all_to_all | solution.py:93
  176.0 7.2 %copy-start.5 = (bf16[2,8,4,1024]{3,2,1,0:T(4,128)(2,1)S(1)}, bf16[2,8,4,1024]{3,2,1,0:T(4,128)(2,1)}, u32[]{:S(2)}) copy-start(bf16[2,8,4,1024]{3,2,1,0:T(4,128)(2,1)} %param.9) | copy-start | bytes 393220
  176.0 9.4 %copy-start.8 = (bf16[2,8,4,128]{3,2,1,0:T(4,128)(2,1)S(1)}, bf16[2,8,4,128]{3,2,1,0:T(4,128)(2,1)}, u32[]{:S(2)}) copy-start(bf16[2,8,4,128]{3,2,1,0:T(4,128)(2,1)} %param.10) | copy-start | bytes 49156
  176.0 68.0 %all-to-all-start = ((bf16[32,5,64,128]{3,2,1,0:T(8,128)(2,1)}), bf16[32,5,64,128]{3,2,1,0:T(8,128)(2,1)}, u32[]{:S(2)}, u32[]{:S(2)}) async-start(bf16[32,5,64,128]{3,2,1,0:T(8,128)(2,1)} %bitcast.230), calls=%async_computation | async-start | bytes 5242880 | tf_op jit(solution)/shard_map/all_to_all | solution.py:94
  183.0 155.8 %all-gather.2.cloned.1.call-start = ((), (), s32[]{:S(2)}) async-start(), calls=%async_computation.3 | async-start | bytes 4325376 | tf_op jit(solution)/shard_map/all_gather | solution.py:124
  254.4 1.5 copy-start.4
  254.5 5.5 %copy-start.3 = (bf16[2,5120,128]{2,1,0:T(8,128)(2,1)}, bf16[2,5120,128]{2,1,0:T(8,128)(2,1)S(1)}, u32[]{:S(2)}) copy-start(bf16[2,5120,128]{2,1,0:T(8,128)(2,1)S(1)} %get-tuple-element.13) | copy-start | bytes 7864324
  254.5 1.1 copy-start.6
  259.9 78.9 %copy-start.7 = (bf16[1024,256]{1,0:T(8,128)(2,1)S(1)}, bf16[1024,256]{1,0:T(8,128)(2,1)}, u32[]{:S(2)}) copy-start(bf16[1024,256]{1,0:T(8,128)(2,1)} %param.14) | copy-start | bytes 1572868
  261.5 115.2 %reduce-scatter.2.cloned.1.call-start = ((), (), s32[]{:S(2)}) async-start(), calls=%async_computation.4 | async-start | bytes 1179648 | tf_op jit(solution)/shard_map/reduce_scatter | solution.py:128
Sparse Core Ops, SparseCore 0:
  261.7 77.1 all-gather.1
  343.4 33.2 reduce-scatter.1
where the time goes:
time: 391 us; the launch traced here: 384 us
  waiting for transfers between devices  220 us (56%)
  other arithmetic  88.5 us (23%)
  local copies, waits for them, and re-layouts  31.9 us (8%)
  starting transfers between devices  18.9 us (5%)
  between operations  14.4 us (4%)
  matrix products  9.47 us (2%)
    all_gather x1, waiting for transfers between devices, local(): lax.all_gather(attention_rows, 'dp', axis=0, tiled=True)  77.2 us
    another operation x6, other arithmetic  74.9 us
    all_to_all x1, waiting for transfers between devices, local(): lax.all_to_all(send_keys, 'dp', split_axis=0, concat_axis=0, tiled=True)  56.3 us
    all_to_all x1, waiting for transfers between devices, local(): lax.all_to_all(send_values, 'dp', split_axis=0, concat_axis=0, tiled=True)  53.4 us
    reduce_scatter x1, waiting for transfers between devices, local(): lax.psum_scatter(partial_out.astype(jnp.bfloat16), 'tp', scatter_dimensio...  33.4 us
    all_to_all x1, starting transfers between devices, local(): lax.all_to_all(send_keys, 'dp', split_axis=0, concat_axis=0, tiled=True)  11.6 us
  transfers between devices with their start and end apart: 4, of which 4 were waited for; matrix products, arithmetic and copies ran while one was open for 3% of the time, Pallas kernels for 0%

commit v1 on v0

v1 whole, which is shorter than its diff:
```python
import functools
import math

import jax
import jax.numpy as jnp
from jax import lax
from jax.experimental import pallas as pl
from jax.experimental.pallas import tpu as pltpu
from jax.sharding import PartitionSpec as P

MESH = pl.DeviceIdType.MESH
BF = jnp.bfloat16
F32 = jnp.float32
I32 = jnp.int32

NZ, NX, NT = 8, 4, 8
HD = 128
QPK = 8
PAGE = 64
PAGES = 80
POOL = 160
SPAN = PAGES * PAGE

FULL = (70, 50, 30, 10)
XFULL = 40
LEVELS = (
    ((38, 29, 19, 8), 38),
    ((44, 33, 23, 9), 40),
    (FULL, XFULL),
)
OWN = 20
PLUS = (20, 90, 140, 170)
MINUS = (180, 250, 300, 330)
ZROOM = 340
SEND_MINUS = 70
CHUNKS = ((0, 0, 32), (0, 32, 32), (1, 0, 32), (1, 32, 16), (1, 48, 16))


def dot(a, b, dims, precision=None):
    return lax.dot_general(a, b, (dims, ((), ())), precision=precision, preferred_element_type=F32)


def tables_kernel(len_ref, assign_ref, bt_ref, t3_ref, t12_ref, lens_ref, level_ref, raw, longs, src_s, used_s, list_s):
    me = lax.axis_index("dp")
    z, x = me // NX, me % NX
    raw[...] = jnp.zeros_like(raw)
    for s in range(64):
        a = assign_ref[s]
        raw[s : s + 1, 0:PAGES] = bt_ref[pl.ds(a, 1), :]
        longs[s : s + 1, :] = jnp.full((1, 128), len_ref[a], I32)

    shape = (64, 128)
    slot = lax.broadcasted_iota(I32, shape, 0)
    lane = lax.broadcasted_iota(I32, shape, 1)
    page = raw[...]
    src = (page * 26215) >> 22
    loc = (page - src * POOL).astype(F32)
    used = jnp.where((lane < PAGES) & (lane * PAGE < longs[...]), 1, 0)
    src = jnp.where(used == 1, src, 1000)
    src_s[...] = src

    tri = jnp.where(lax.broadcasted_iota(I32, (128, 128), 0) < lax.broadcasted_iota(I32, (128, 128), 1), 1.0, 0.0).astype(BF)
    bi, bj = lax.broadcasted_iota(I32, (64, 64), 0), lax.broadcasted_iota(I32, (64, 64), 1)
    blocks = jnp.where((bi // 8 == bj // 8) & (bj < bi), 1.0, 0.0).astype(BF)

    def ranks(mask):
        total = jnp.broadcast_to(jnp.sum(mask, axis=1, keepdims=True), shape)
        return dot(mask.astype(BF), tri, ((1,), (0,))) + dot(blocks, total.astype(BF), ((1,), (0,)))

    count = jnp.zeros(shape, F32)
    for e in range(32):
        total = jnp.sum(jnp.where(src == e, 1.0, 0.0), axis=1, keepdims=True)
        count = jnp.where(lane == e, total, count)
    dist = (slot // 8 - lane // NX) & 7
    at = [jnp.sum(jnp.where((dist == k) & (lane < 32), count, 0.0), axis=0, keepdims=True) for k in range(8)]
    p4 = jnp.floor((at[4] + 1.0) * 0.5)
    m4 = at[4] - p4
    plus = [None] * 5
    minus = [None] * 5
    plus[4], minus[4] = p4, m4
    for j in (3, 2, 1):
        plus[j] = plus[j + 1] + at[j]
        minus[j] = minus[j + 1] + at[8 - j]
    nil = jnp.zeros_like(p4)
    offset = [nil, plus[2], plus[3], plus[4], nil, minus[4], minus[3], minus[2]]

    by_x = jnp.zeros(shape, F32)
    for k in range(NX):
        total = jnp.sum(jnp.where((lane & 3) == k, count, 0.0), axis=1, keepdims=True)
        by_x = jnp.where(lane == k, total, by_x)
    pairs = by_x + pltpu.roll(by_x, 1, 0)
    pairs = jnp.where((slot % 2 == 1) & (lane != (slot // 2) % NX), pairs, 0.0)
    x_most = jnp.max(pairs)
    needs = [(jnp.maximum(jnp.max(plus[j]), jnp.max(minus[j])), j - 1) for j in (1, 2, 3, 4)]
    level = jnp.int32(0)
    for caps, x_cap in LEVELS[:-1]:
        over = jnp.where(x_most > float(x_cap), 1, 0)
        for need, j in needs:
            over = jnp.maximum(over, jnp.where(need > float(caps[j]), 1, 0))
        level = level + over
    level_ref[0] = level

    def column(row, e):
        return jnp.sum(jnp.where(lax.broadcasted_iota(I32, (1, 128), 1) == e, row, 0.0), axis=1, keepdims=True)

    mine = src == me
    rank = ranks(jnp.where(mine, 1.0, 0.0))
    away = (slot // 8 - z) & 7
    half = column(p4, me)
    place = rank
    for k in range(1, 8):
        base = OWN if k < 4 else OWN + SEND_MINUS
        value = column(offset[k], me) + rank + float(base)
        if k == 4:
            value = jnp.where(rank < half, rank + float(OWN), rank - half + float(OWN + SEND_MINUS))
        place = jnp.where(away == k, value, place)
    place = jnp.where(mine, place, -1.0)

    def first_list(g, _):
        rows = []
        for i in range(8):
            k = (g * 8 + i).astype(F32)
            rows.append(jnp.sum(jnp.where(place == k, loc, 0.0), axis=0, keepdims=True))
        list_s[pl.ds(pl.multiple_of(g * 8, 8), 8), :] = jnp.concatenate(rows, axis=0)
        return 0

    lax.fori_loop(0, 20, first_list, 0)
    ones = jnp.ones((8, 128), F32)
    t12_ref[0:8, :] = dot(ones, list_s[...], ((1,), (1,)), lax.Precision.HIGHEST).astype(I32)

    row8 = pl.ds(pl.multiple_of(z * 8, 8), 8)
    src_r = src_s[row8, :]
    marks = jnp.concatenate([jnp.where(src_r == zs * NX + x, 1.0, 0.0) for zs in range(NZ)], axis=0)
    rank = ranks(marks)
    off8 = jnp.concatenate(offset, axis=0)
    k8 = lax.broadcasted_iota(I32, (8, 128), 0)
    e8 = lax.broadcasted_iota(I32, (8, 128), 1)
    here = (e8 & 3) == x
    off_e = jnp.sum(jnp.where(here & (k8 == ((z - e8 // NX) & 7)), off8, 0.0), axis=0, keepdims=True)
    half_e = jnp.where(here[0:1], p4, 0.0)
    through = jnp.zeros((8, 128), F32)
    for zs in range(NZ):
        r = rank[zs * 8 : zs * 8 + 8]
        pick = (e8[0:1] // NX) == zs
        off = jnp.sum(jnp.where(pick, off_e, 0.0), axis=1, keepdims=True)
        half = jnp.sum(jnp.where(pick, half_e, 0.0), axis=1, keepdims=True)
        d = jnp.broadcast_to((z - zs) & 7, (8, 128))
        value = r
        for k in range(1, 8):
            if k == 4:
                v = jnp.where(r < half, r + float(PLUS[3]), r - half + float(MINUS[3]))
            else:
                v = off + r + float(PLUS[k - 1] if k < 4 else MINUS[7 - k])
            value = jnp.where(d == k, v, value)
        through = through + marks[zs * 8 : zs * 8 + 8] * value

    used_r = src_r < 32
    odd = (k8 & 1) == 1
    order = jnp.zeros((8, 128), F32)
    for k in range(NX):
        mark = jnp.where(used_r & ((src_r & 3) == k), 1.0, 0.0)
        total = jnp.broadcast_to(jnp.sum(mark, axis=1, keepdims=True), (8, 128))
        r = dot(mark.astype(BF), tri, ((1,), (0,))) + jnp.where(odd, pltpu.roll(total, 1, 0), 0.0)
        order = order + mark * r
    order_i = order.astype(I32)
    t3_ref[...] = jnp.where(used_r, ((src_r - x) & 3) * XFULL + order_i, 0)
    lens_ref[...] = longs[row8, :]
    goes = ((k8 // 2 - x) & 3) * XFULL + order_i
    goes = jnp.where(used_r & ((src_r & 3) == x), goes, -1)

    def second_list(g, _):
        rows = []
        for i in range(8):
            rows.append(jnp.sum(jnp.where(goes == g * 8 + i, through, 0.0), axis=0, keepdims=True))
        list_s[pl.ds(pl.multiple_of(g * 8, 8), 8), :] = jnp.concatenate(rows, axis=0)
        return 0

    lax.fori_loop(0, 20, second_list, 0)
    t12_ref[8:16, :] = dot(ones, list_s[...], ((1,), (1,)), lax.Precision.HIGHEST).astype(I32)


def make_tables(mem_len, assign, block_table):
    smem = pl.BlockSpec(memory_space=pltpu.SMEM)
    vmem = pl.BlockSpec(memory_space=pltpu.VMEM)
    return pl.pallas_call(
        tables_kernel,
        out_shape=(
            jax.ShapeDtypeStruct((8, 128), I32),
            jax.ShapeDtypeStruct((16, 160), I32),
            jax.ShapeDtypeStruct((8, 128), I32),
            jax.ShapeDtypeStruct((1,), I32),
        ),
        in_specs=[smem, smem, vmem],
        out_specs=(vmem, vmem, vmem, smem),
        scratch_shapes=[
            pltpu.VMEM((64, 128), I32),
            pltpu.VMEM((64, 128), I32),
            pltpu.VMEM((64, 128), I32),
            pltpu.VMEM((64, 128), I32),
            pltpu.VMEM((160, 128), F32),
        ],
    )(mem_len, assign, block_table)


def handoff_kernel(caps, x_cap, *refs):
    n = len(CHUNKS)
    it = iter(refs)
    t3, t12, lens, q_ref, nk_ref, nv_ref, kp_hbm, vp_hbm, w_hbm = (next(it) for _ in range(9))
    lo_ref, ko_hbm, vo_hbm = (next(it) for _ in range(3))
    pools = (next(it), next(it))
    staged = (next(it), next(it))
    zs = [next(it) for _ in range(n)]
    zb = [next(it) for _ in range(n)]
    xs = [next(it) for _ in range(n)]
    xb = [next(it) for _ in range(n)]
    probs, att, wbuf, abuf, part, rbuf, fin_s, fin = (next(it) for _ in range(8))
    local_sem, z_send, z_recv, x_send, x_recv, w_send, w_recv, a_send, a_recv, r_send, r_recv, f_send, f_recv = it

    me, tp = lax.axis_index("dp"), lax.axis_index("tp")
    z, x = me // NX, me % NX
    z_to = [{"dp": ((z + 1) % NZ) * NX + x}, {"dp": ((z + NZ - 1) % NZ) * NX + x}]
    x_to = [{"dp": z * NX + (x + r) % NX} for r in range(NX)]
    t_to = [{"tp": (tp + r) % NT} for r in range(NT)]

    loads = [
        pltpu.make_async_copy(kp_hbm, pools[0], local_sem.at[0]),
        pltpu.make_async_copy(vp_hbm, pools[1], local_sem.at[1]),
        pltpu.make_async_copy(w_hbm, wbuf.at[0], local_sem.at[2]),
    ]
    for c in loads:
        c.start()
    barrier = pltpu.get_barrier_semaphore()
    peers = z_to + x_to[1:] + t_to[1:]
    for d in peers:
        pl.semaphore_signal(barrier, inc=1, device_id=d, device_id_type=MESH)

    def remote(src, dst, ss, rs, to):
        return pltpu.make_async_remote_copy(
            src_ref=src, dst_ref=dst, send_sem=ss, recv_sem=rs, device_id=to, device_id_type=MESH
        )

    sent = []

    def z_copy(c, d, j):
        base = (PLUS, MINUS)[d]
        if j == 1:
            src = zs[c].at[pl.ds(d * SEND_MINUS, caps[0])]
        else:
            src = zb[c].at[pl.ds(base[j - 2], caps[j - 1])]
        return remote(src, zb[c].at[pl.ds(base[j - 1], caps[j - 1])], z_send.at[c, d, j - 1], z_recv.at[c, d, j - 1], z_to[d])

    def z_start(c, j):
        for d in range(2):
            cp = z_copy(c, d, j)
            cp.start()
            sent.append(cp)

    def x_copy(c, r):
        return remote(
            xs[c].at[pl.ds((r - 1) * XFULL, x_cap)],
            xb[c].at[pl.ds((NX - r) * XFULL, x_cap)],
            x_send.at[c, r - 1],
            x_recv.at[c, r - 1],
            x_to[r],
        )

    def pack_pool(which):
        mine = [(c, r0, rows) for c, (w, r0, rows) in enumerate(CHUNKS) if w == which]
        pool = pools[which]

        def body(first, dst, place, k, _):
            got = pool[t12[0, first + k]]
            for c, r0, rows in mine:
                dst[c][place + k] = got[r0 : r0 + rows]
            return 0

        lax.fori_loop(0, OWN, functools.partial(body, 0, zb, 0), 0, unroll=4)
        lax.fori_loop(0, caps[0], functools.partial(body, OWN, zs, 0), 0, unroll=2)
        lax.fori_loop(0, caps[0], functools.partial(body, OWN + SEND_MINUS, zs, SEND_MINUS), 0, unroll=2)

    def pack_row(c):
        def body(first, dst, place, k, _):
            dst[place + k] = zb[c][t12[8, first + k]]
            return 0

        for r in (2, 1, 3):
            lax.fori_loop(0, x_cap, functools.partial(body, r * XFULL, xs[c], (r - 1) * XFULL), 0, unroll=2)
            cp = x_copy(c, r)
            cp.start()
            sent.append(cp)
        lax.fori_loop(0, XFULL, functools.partial(body, 0, xb[c], 0), 0, unroll=4)

    def place_pages(c):
        which, r0, rows = CHUNKS[c]
        token = lax.broadcasted_iota(I32, (rows, HD), 0)
        for s in range(2):

            def body(p, _):
                got = xb[c][t3[2 * x + s, p]]
                left = lens[2 * x + s, 0] - p * PAGE - r0
                got = jnp.where(token < left, got.astype(F32), 0.0).astype(BF)
                staged[which][s, pl.ds(pl.multiple_of(p * PAGE + r0, 16), rows), :] = got
                return 0

            lax.fori_loop(0, PAGES, body, 0, unroll=4)

    scale = 1.0 / math.sqrt(HD)
    tile = 512

    def queries_of(s):
        rows = q_ref[s * 32 : (s + 1) * 32, :]
        return jnp.concatenate([rows[:, h * HD : (h + 1) * HD] for h in range(QPK)], axis=0)

    def fresh_scores(s):
        sc = dot(queries_of(s), nk_ref[s * 32 : (s + 1) * 32, :], ((1,), (1,))) * scale
        r = lax.broadcasted_iota(I32, sc.shape, 0) % 32
        u = lax.broadcasted_iota(I32, sc.shape, 1)
        ok = (r // 4 == u // 4) & (u % 4 <= r % 4)
        return jnp.where(ok, sc, -jnp.inf)

    def tile_scores(s, q, i, length):
        keys = staged[0][s, pl.ds(pl.multiple_of(i * tile, tile), tile), :]
        sc = dot(q, keys, ((1,), (1,))) * scale
        pos = lax.broadcasted_iota(I32, sc.shape, 1) + i * tile
        return jnp.where(pos < length, sc, -jnp.inf)

    def find_max(s):
        q = queries_of(s)
        length = lens[2 * x + s, 0]

        def body(i, m):
            sc = tile_scores(s, q, i, length)
            for k in range(tile // 128):
                m = jnp.maximum(m, sc[:, k * 128 : (k + 1) * 128])
            return m

        m = lax.fori_loop(0, SPAN // tile, body, jnp.full((256, 128), -jnp.inf, F32))
        top = jnp.maximum(jnp.max(m, axis=1, keepdims=True), jnp.max(fresh_scores(s), axis=1, keepdims=True))
        att[s, 0] = jnp.broadcast_to(top, (256, 128))

    def weigh(s):
        q = queries_of(s)
        length = lens[2 * x + s, 0]
        top = att[s, 0][:, 0:1]

        def body(i, t):
            w = jnp.exp(tile_scores(s, q, i, length) - top)
            probs[s, :, pl.ds(pl.multiple_of(i * tile, tile), tile)] = w.astype(BF)
            for k in range(tile // 128):
                t = t + w[:, k * 128 : (k + 1) * 128]
            return t

        t = lax.fori_loop(0, SPAN // tile, body, jnp.zeros((256, 128), F32))
        fresh = jnp.exp(fresh_scores(s) - top)
        total = jnp.sum(t, axis=1, keepdims=True) + jnp.sum(fresh, axis=1, keepdims=True)
        att[s, 0] = jnp.broadcast_to(total, (256, 128))
        att[s, 1] = dot(fresh.astype(BF), nv_ref[s * 32 : (s + 1) * 32, :], ((1,), (0,)))

    def finish(s):
        acc = att[s, 1]

        def body(i, a):
            at = pl.ds(pl.multiple_of(i * 1024, 1024), 1024)
            return a + dot(probs[s, :, at], staged[1][s, at, :], ((1,), (0,)))

        acc = lax.fori_loop(0, SPAN // 1024, body, acc)
        rows = (acc / att[s, 0]).astype(BF)
        for h in range(QPK):
            abuf[0, s * 32 : (s + 1) * 32, h * HD : (h + 1) * HD] = rows[h * 32 : (h + 1) * 32, :]

    half = wbuf.shape[1] // 2

    def w_copy(i):
        src, dst, r = (
            (wbuf.at[0], wbuf.at[3], 1),
            (wbuf.at[0], wbuf.at[1], 3),
            (wbuf.at[3, pl.ds(0, half)], wbuf.at[2, pl.ds(0, half)], 1),
            (wbuf.at[1, pl.ds(half, half)], wbuf.at[2, pl.ds(half, half)], 3),
        )[i]
        return remote(src, dst, w_send.at[i], w_recv.at[i], x_to[r])

    def w_start(i):
        cp = w_copy(i)
        cp.start()
        sent.append(cp)

    pl.semaphore_wait(barrier, len(peers))
    loads[0].wait()
    pack_pool(0)
    z_start(0, 1)
    z_start(1, 1)
    loads[2].wait()
    w_start(0)
    w_start(1)
    loads[1].wait()
    pack_pool(1)

    k_last = max(c for c, ch in enumerate(CHUNKS) if ch[0] == 0)
    work = [functools.partial(find_max, 0), functools.partial(find_max, 1), functools.partial(weigh, 0), functools.partial(weigh, 1)]
    flush = []
    k_ready = False
    for r in range(1, n + 6):
        for c in range(max(0, r - 4), min(n, r)):
            j = r - c
            for d in range(2):
                z_copy(c, d, j).wait_recv()
            if j < 4:
                z_start(c, j + 1)
        if r + 1 < n:
            z_start(r + 1, 1)
        if r == 2:
            w_copy(0).wait_recv()
            w_copy(1).wait_recv()
            w_start(2)
            w_start(3)
        if 0 <= r - 4 < n:
            pack_row(r - 4)
        if k_ready and work:
            if r >= n + 3:
                while work:
                    work.pop(0)()
            else:
                work.pop(0)()
        if 0 <= r - 5 < n:
            c = r - 5
            for i in (1, 2, 3):
                x_copy(c, i).wait_recv()
            place_pages(c)
            if c == k_last:
                k_ready = True
                out = pltpu.make_async_copy(staged[0], ko_hbm, local_sem.at[3])
                out.start()
                flush.append(out)
    out = pltpu.make_async_copy(staged[1], vo_hbm, local_sem.at[4])
    out.start()
    flush.append(out)

    def a_copy(s, d, j):
        rows = pl.ds(s * 32, 32)
        here = (j - 1) if d == 0 else (9 - j) % 8
        there = j if d == 0 else 8 - j
        return remote(abuf.at[here, rows], abuf.at[there, rows], a_send.at[s, d, j - 1], a_recv.at[s, d, j - 1], z_to[d])

    def a_start(s, d, j):
        cp = a_copy(s, d, j)
        cp.start()
        sent.append(cp)

    for s in range(2):
        finish(s)
        for d in range(2):
            a_start(s, d, 1)

    w_copy(2).wait_recv()
    w_copy(3).wait_recv()

    def block_copy(r):
        return remote(part.at[r], rbuf.at[tp], r_send.at[r], r_recv.at[tp], {"tp": (z + NZ - r) % NZ})

    def project(r):
        rows = abuf[r]
        for k in range(NX):
            part[r, :, k * 256 : (k + 1) * 256] = dot(rows, wbuf[k], ((1,), (0,))).astype(BF)
        target = (z + NZ - r) % NZ

        @pl.when(target != tp)
        def _():
            block_copy(r).start()

        @pl.when(target == tp)
        def _():
            rbuf[tp] = part[r]

    project(0)
    for j in (1, 2, 3, 4):
        for s in range(2):
            for d in range(2):
                if j < 4 or s == d:
                    a_copy(s, d, j).wait_recv()
                if j < 3 or (j == 3 and s == d):
                    a_start(s, d, j + 1)
        project(j)
        if j < 4:
            project(8 - j)

    total = jnp.zeros((64, 1024), F32)
    for t in range(NT):

        @pl.when(t != tp)
        def _():
            remote(part.at[0], rbuf.at[t], r_send.at[0], r_recv.at[t], t_to[1]).wait_recv()

    for t in range(NT):
        total = total + rbuf[t].astype(F32)
    total = total.astype(BF)
    rows = pl.ds(pl.multiple_of(x * 64, 64), 64)
    fin[rows, :] = total[:, 0:256]
    for k in range(1, NX):
        fin_s[k - 1] = total[:, k * 256 : (k + 1) * 256]
        cp = remote(fin_s.at[k - 1], fin.at[rows], f_send.at[k - 1], f_recv.at[k - 1], x_to[k])
        cp.start()
        sent.append(cp)
    for k in range(1, NX):
        from_rows = pl.ds(pl.multiple_of(((x + NX - k) % NX) * 64, 64), 64)
        remote(fin_s.at[k - 1], fin.at[from_rows], f_send.at[k - 1], f_recv.at[k - 1], x_to[k]).wait_recv()
    lo_ref[...] = fin[...]
    for r in range(NZ):

        @pl.when((z + NZ - r) % NZ != tp)
        def _():
            block_copy(r).wait_send()

    for cp in sent:
        cp.wait_send()
    for cp in flush:
        cp.wait()


def handoff(level, t3, t12, lens, q, nk, nv, key_pool, value_pool, out_weight):
    caps, x_cap = LEVELS[level]
    n = len(CHUNKS)
    smem = pl.BlockSpec(memory_space=pltpu.SMEM)
    vmem = pl.BlockSpec(memory_space=pltpu.VMEM)
    hbm = pl.BlockSpec(memory_space=pl.ANY)
    dma = pltpu.SemaphoreType.DMA
    scratch = [pltpu.VMEM((POOL, PAGE, HD), BF)] * 2 + [pltpu.VMEM((2, SPAN, HD), BF)] * 2
    for pages in (2 * SEND_MINUS, ZROOM, 3 * XFULL, 4 * XFULL):
        scratch += [pltpu.VMEM((pages, rows, HD), BF) for _, _, rows in CHUNKS]
    scratch += [
        pltpu.VMEM((2, 256, SPAN), BF),
        pltpu.VMEM((2, 2, 256, 128), F32),
        pltpu.VMEM((NX, 1024, 256), BF),
        pltpu.VMEM((NZ, 64, 1024), BF),
        pltpu.VMEM((NZ, 64, 1024), BF),
        pltpu.VMEM((NT, 64, 1024), BF),
        pltpu.VMEM((3, 64, 256), BF),
        pltpu.VMEM((256, 256), BF),
        dma((5,)),
        dma((n, 2, 4)),
        dma((n, 2, 4)),
        dma((n, 3)),
        dma((n, 3)),
        dma((4,)),
        dma((4,)),
        dma((2, 2, 4)),
        dma((2, 2, 4)),
        dma((NZ,)),
        dma((NT,)),
        dma((3,)),
        dma((3,)),
    ]
    return pl.pallas_call(
        functools.partial(handoff_kernel, caps, x_cap),
        out_shape=(
            jax.ShapeDtypeStruct((256, 256), BF),
            jax.ShapeDtypeStruct((2, SPAN, HD), BF),
            jax.ShapeDtypeStruct((2, SPAN, HD), BF),
        ),
        in_specs=[smem] * 3 + [vmem] * 3 + [hbm] * 3,
        out_specs=(vmem, hbm, hbm),
        scratch_shapes=scratch,
        compiler_params=pltpu.CompilerParams(
            collective_id=level, has_side_effects=True, vmem_limit_bytes=58 * 2**20
        ),
    )(t3, t12, lens, q, nk, nv, key_pool, value_pool, out_weight)


def local(queries, new_keys, new_values, key_pool, value_pool, out_weight, mem_len, assign, block_table):
    t3, t12, lens, level = make_tables(mem_len, assign, block_table)
    q = queries.reshape(64, 1024)
    nk = new_keys.reshape(64, HD)
    nv = new_values.reshape(64, HD)
    branches = [functools.partial(handoff, i) for i in range(len(LEVELS))]
    return lax.switch(level[0], branches, t3, t12, lens, q, nk, nv, key_pool, value_pool, out_weight)


def solution(mesh):
    placed = (
        P("dp", None, None, "tp"),
        P("dp", None, None, "tp"),
        P("dp", None, None, "tp"),
        P("dp", None, "tp"),
        P("dp", None, "tp"),
        P("tp", "dp"),
        P(),
        P(),
        P(),
    )
    return jax.shard_map(
        local,
        mesh=mesh,
        in_specs=placed,
        out_specs=(P("tp", "dp"), P("dp", None, "tp"), P("dp", None, "tp")),
        check_vma=False,
    )
```

time: 391 us -> 156 us (0.40)
  the two profiles are of different devices: /device:TPU:4 before, /device:TPU:16 now
where the time goes in v1:
time: 156 us
  Pallas kernels  149 us (96%)
  local copies, waits for them, and re-layouts  5.77 us (4%)
    pallas_call x1, Pallas kernels, handoff(): pl.pallas_call(functools.partial(handoff_kernel, caps, x_cap), out_shape=...  145 us
    unnamed x5, local copies, waits for them, and re-layouts  4.83 us
    pallas_call x1, Pallas kernels, make_tables(): pl.pallas_call(tables_kernel, out_shape=(jax.ShapeDtypeStruct((8, 128), I...  3.51 us

profile of v1, /device:TPU:16, one launch (start us, length us, event | category | flops | bytes accessed | tf_op | source)
XLA Modules:
  0.0 156.0 jit_solution(12042000518767498738)
XLA Ops:
  0.6 3.5 %shard_map.121 = (s32[8,128]{1,0:T(8,128)S(1)}, s32[16,160]{1,0:T(8,128)S(1)}, s32[8,128]{1,0:T(8,128)S(1)}, s32[1]{0:T(128)}) custom-call(s32[64]{0:T(128)} %len_ref.1, s32[64]{0:T(128)} %assign_ref.1, s32[64,80]{1,0:T(8,128)} %bt_ref.1), custom_call_target="tpu_custom_call" | custom-call | tf_op jit(solution)/shard_map/pallas_call | solution.py:185
  4.8 0.9 reshape.18
  5.7 145.4 %conditional.1 = ((bf16[256,256]{1,0:T(8,128)(2,1)S(1)}, bf16[2,5120,128]{2,1,0:T(8,128)(2,1)S(1)}, bf16[2,5120,128]{2,1,0:T(8,128)(2,1)})) conditional(s32[]{:T(128)} %bitcast, (s32[8,128]{1,0:T(8,128)S(1)}, s32[16,160]{1,0:T(8,128)S(1)}, s32[8,128]{1,0:T(8,128)S(1)}, bf16[64,1024]{1,0:T(8,128)(2,1)S(1)}, ...), branch_computations={%region_0.0_spmd, %region_1.0_spmd, %region_2.0_spmd} | conditional | bytes 8 | solution.py:574
  5.8 145.2 %branch_0_fun.1 = (bf16[256,256]{1,0:T(8,128)(2,1)S(1)}, bf16[2,5120,128]{2,1,0:T(8,128)(2,1)S(1)}, bf16[2,5120,128]{2,1,0:T(8,128)(2,1)}) custom-call(s32[8,128]{1,0:T(8,128)S(1)} %get-tuple-element.54.refs_0_, s32[16,160]{1,0:T(8,128)S(1)} %get-tuple-element.55.refs_1_, s32[8,128]{1,0:T(8,128)S(1)} %get-tuple-element.56.refs_2_, ...), custom_call_target="tpu_custom_call" | custom-call | tf_op jit(solution)/shard_map/cond/branch_0_fun/pallas_call | solution.py:552
  151.2 0.7 copy.33
  151.9 0.0 copy-start
  151.9 1.5 copy.34
  153.3 1.2 copy-done
  154.5 1.5 copy.35
Async XLA Ops:
  151.9 2.7 %copy-start = (bf16[2,5120,128]{2,1,0:T(8,128)(2,1)S(1)}, bf16[2,5120,128]{2,1,0:T(8,128)(2,1)}, u32[]{:S(2)}) copy-start(bf16[2,5120,128]{2,1,0:T(8,128)(2,1)} %get-tuple-element.118) | copy-start | bytes 7864324

commit v2 on v1

--- a/solution.py
+++ b/solution.py
@@ -21,19 +21,22 @@
 POOL = 160
 SPAN = PAGES * PAGE
 
-FULL = (70, 50, 30, 10)
+FULL = (73, 53, 33, 13)
 XFULL = 40
 LEVELS = (
-    ((38, 29, 19, 8), 38),
-    ((44, 33, 23, 9), 40),
-    (FULL, XFULL),
+    (36, 28, 19, 9),
+    (39, 30, 21, 10),
+    (45, 34, 24, 12),
+    FULL,
 )
 OWN = 20
-PLUS = (20, 90, 140, 170)
-MINUS = (180, 250, 300, 330)
-ZROOM = 340
-SEND_MINUS = 70
-CHUNKS = ((0, 0, 32), (0, 32, 32), (1, 0, 32), (1, 32, 16), (1, 48, 16))
+PLUS = (20, 93, 0, 33)
+MINUS = (146, 219, 46, 79)
+ZROOM = (272, 92)
+XNEAR = 25
+SEND_MINUS = FULL[0]
+LIST = 168
+CHUNKS = tuple((w, r, 16) for w in (0, 1) for r in (0, 16, 32, 48))
 
 
 def dot(a, b, dims, precision=None):
@@ -73,7 +76,13 @@
         count = jnp.where(lane == e, total, count)
     dist = (slot // 8 - lane // NX) & 7
     at = [jnp.sum(jnp.where((dist == k) & (lane < 32), count, 0.0), axis=0, keepdims=True) for k in range(8)]
-    p4 = jnp.floor((at[4] + 1.0) * 0.5)
+    lean = (at[5] + at[6] + at[7] - at[1] - at[2] - at[3]) * 0.25
+    middle = at[4] * 0.5
+    p4 = jnp.clip(
+        jnp.floor(middle + lean + 0.5),
+        jnp.floor(jnp.maximum(middle - 3.0, 0.0)),
+        jnp.minimum(at[4], jnp.ceil(middle) + 3.0),
+    )
     m4 = at[4] - p4
     plus = [None] * 5
     minus = [None] * 5
@@ -84,17 +93,10 @@
     nil = jnp.zeros_like(p4)
     offset = [nil, plus[2], plus[3], plus[4], nil, minus[4], minus[3], minus[2]]
 
-    by_x = jnp.zeros(shape, F32)
-    for k in range(NX):
-        total = jnp.sum(jnp.where((lane & 3) == k, count, 0.0), axis=1, keepdims=True)
-        by_x = jnp.where(lane == k, total, by_x)
-    pairs = by_x + pltpu.roll(by_x, 1, 0)
-    pairs = jnp.where((slot % 2 == 1) & (lane != (slot // 2) % NX), pairs, 0.0)
-    x_most = jnp.max(pairs)
     needs = [(jnp.maximum(jnp.max(plus[j]), jnp.max(minus[j])), j - 1) for j in (1, 2, 3, 4)]
     level = jnp.int32(0)
-    for caps, x_cap in LEVELS[:-1]:
-        over = jnp.where(x_most > float(x_cap), 1, 0)
+    for caps in LEVELS[:-1]:
+        over = jnp.int32(0)
         for need, j in needs:
             over = jnp.maximum(over, jnp.where(need > float(caps[j]), 1, 0))
         level = level + over
@@ -124,7 +126,7 @@
         list_s[pl.ds(pl.multiple_of(g * 8, 8), 8), :] = jnp.concatenate(rows, axis=0)
         return 0
 
-    lax.fori_loop(0, 20, first_list, 0)
+    lax.fori_loop(0, LIST // 8, first_list, 0)
     ones = jnp.ones((8, 128), F32)
     t12_ref[0:8, :] = dot(ones, list_s[...], ((1,), (1,)), lax.Precision.HIGHEST).astype(I32)
 
@@ -156,9 +158,11 @@
 
     used_r = src_r < 32
     odd = (k8 & 1) == 1
-    order = jnp.zeros((8, 128), F32)
-    for k in range(NX):
-        mark = jnp.where(used_r & ((src_r & 3) == k), 1.0, 0.0)
+    apart = (z - (src_r >> 2)) & 7
+    far = (apart >= 3) & (apart <= 5)
+    order = jnp.where(far, float(XNEAR), 0.0)
+    for k in range(2 * NX):
+        mark = jnp.where(used_r & ((src_r & 3) == k // 2) & (far if k % 2 else ~far), 1.0, 0.0)
         total = jnp.broadcast_to(jnp.sum(mark, axis=1, keepdims=True), (8, 128))
         r = dot(mark.astype(BF), tri, ((1,), (0,))) + jnp.where(odd, pltpu.roll(total, 1, 0), 0.0)
         order = order + mark * r
@@ -175,7 +179,7 @@
         list_s[pl.ds(pl.multiple_of(g * 8, 8), 8), :] = jnp.concatenate(rows, axis=0)
         return 0
 
-    lax.fori_loop(0, 20, second_list, 0)
+    lax.fori_loop(0, LIST // 8, second_list, 0)
     t12_ref[8:16, :] = dot(ones, list_s[...], ((1,), (1,)), lax.Precision.HIGHEST).astype(I32)
 
 
@@ -186,7 +190,7 @@
         tables_kernel,
         out_shape=(
             jax.ShapeDtypeStruct((8, 128), I32),
-            jax.ShapeDtypeStruct((16, 160), I32),
+            jax.ShapeDtypeStruct((16, LIST), I32),
             jax.ShapeDtypeStruct((8, 128), I32),
             jax.ShapeDtypeStruct((1,), I32),
         ),
@@ -197,12 +201,12 @@
             pltpu.VMEM((64, 128), I32),
             pltpu.VMEM((64, 128), I32),
             pltpu.VMEM((64, 128), I32),
-            pltpu.VMEM((160, 128), F32),
+            pltpu.VMEM((LIST, 128), F32),
         ],
     )(mem_len, assign, block_table)
 
 
-def handoff_kernel(caps, x_cap, *refs):
+def handoff_kernel(caps, *refs):
     n = len(CHUNKS)
     it = iter(refs)
     t3, t12, lens, q_ref, nk_ref, nv_ref, kp_hbm, vp_hbm, w_hbm = (next(it) for _ in range(9))
@@ -210,7 +214,7 @@
     pools = (next(it), next(it))
     staged = (next(it), next(it))
     zs = [next(it) for _ in range(n)]
-    zb = [next(it) for _ in range(n)]
+    zb = [(next(it), next(it)) for _ in range(n)]
     xs = [next(it) for _ in range(n)]
     xb = [next(it) for _ in range(n)]
     probs, att, wbuf, abuf, part, rbuf, fin_s, fin = (next(it) for _ in range(8))
@@ -246,8 +250,9 @@
         if j == 1:
             src = zs[c].at[pl.ds(d * SEND_MINUS, caps[0])]
         else:
-            src = zb[c].at[pl.ds(base[j - 2], caps[j - 1])]
-        return remote(src, zb[c].at[pl.ds(base[j - 1], caps[j - 1])], z_send.at[c, d, j - 1], z_recv.at[c, d, j - 1], z_to[d])
+            src = zb[c][(j - 2) // 2].at[pl.ds(base[j - 2], caps[j - 1])]
+        dst = zb[c][(j - 1) // 2].at[pl.ds(base[j - 1], caps[j - 1])]
+        return remote(src, dst, z_send.at[c, d, j - 1], z_recv.at[c, d, j - 1], z_to[d])
 
     def z_start(c, j):
         for d in range(2):
@@ -255,12 +260,15 @@
             cp.start()
             sent.append(cp)
 
-    def x_copy(c, r):
+    spans = ((0, XNEAR), (XNEAR, XFULL - XNEAR))
+
+    def x_copy(c, r, far):
+        first, pages = spans[far]
         return remote(
-            xs[c].at[pl.ds((r - 1) * XFULL, x_cap)],
-            xb[c].at[pl.ds((NX - r) * XFULL, x_cap)],
-            x_send.at[c, r - 1],
-            x_recv.at[c, r - 1],
+            xs[c].at[pl.ds((r - 1) * XFULL + first, pages)],
+            xb[c].at[pl.ds((NX - r) * XFULL + first, pages)],
+            x_send.at[c, far, r - 1],
+            x_recv.at[c, far, r - 1],
             x_to[r],
         )
 
@@ -274,21 +282,26 @@
                 dst[c][place + k] = got[r0 : r0 + rows]
             return 0
 
-        lax.fori_loop(0, OWN, functools.partial(body, 0, zb, 0), 0, unroll=4)
+        near = [z[0] for z in zb]
+
+        lax.fori_loop(0, OWN, functools.partial(body, 0, near, 0), 0, unroll=4)
         lax.fori_loop(0, caps[0], functools.partial(body, OWN, zs, 0), 0, unroll=2)
         lax.fori_loop(0, caps[0], functools.partial(body, OWN + SEND_MINUS, zs, SEND_MINUS), 0, unroll=2)
 
-    def pack_row(c):
+    def pack_row(c, far):
+        start, pages = spans[far]
+
         def body(first, dst, place, k, _):
-            dst[place + k] = zb[c][t12[8, first + k]]
+            dst[place + k] = zb[c][far][t12[8, first + k]]
             return 0
 
         for r in (2, 1, 3):
-            lax.fori_loop(0, x_cap, functools.partial(body, r * XFULL, xs[c], (r - 1) * XFULL), 0, unroll=2)
-            cp = x_copy(c, r)
+            put = functools.partial(body, r * XFULL + start, xs[c], (r - 1) * XFULL + start)
+            lax.fori_loop(0, pages, put, 0, unroll=5)
+            cp = x_copy(c, r, far)
             cp.start()
             sent.append(cp)
-        lax.fori_loop(0, XFULL, functools.partial(body, 0, xb[c], 0), 0, unroll=4)
+        lax.fori_loop(0, pages, functools.partial(body, start, xb[c], start), 0, unroll=5)
 
     def place_pages(c):
         which, r0, rows = CHUNKS[c]
@@ -396,10 +409,9 @@
     pack_pool(1)
 
     k_last = max(c for c, ch in enumerate(CHUNKS) if ch[0] == 0)
-    work = [functools.partial(find_max, 0), functools.partial(find_max, 1), functools.partial(weigh, 0), functools.partial(weigh, 1)]
+    work = [functools.partial(f, s) for f in (find_max, weigh) for s in range(2)]
     flush = []
-    k_ready = False
-    for r in range(1, n + 6):
+    for r in range(1, n + 5):
         for c in range(max(0, r - 4), min(n, r)):
             j = r - c
             for d in range(2):
@@ -414,23 +426,21 @@
             w_start(2)
             w_start(3)
         if 0 <= r - 4 < n:
-            pack_row(r - 4)
-        if k_ready and work:
-            if r >= n + 3:
-                while work:
-                    work.pop(0)()
-            else:
-                work.pop(0)()
+            pack_row(r - 4, 1)
+        if 0 <= r - 2 < n:
+            pack_row(r - 2, 0)
         if 0 <= r - 5 < n:
             c = r - 5
-            for i in (1, 2, 3):
-                x_copy(c, i).wait_recv()
+            for far in range(2):
+                for i in (1, 2, 3):
+                    x_copy(c, i, far).wait_recv()
             place_pages(c)
             if c == k_last:
-                k_ready = True
                 out = pltpu.make_async_copy(staged[0], ko_hbm, local_sem.at[3])
                 out.start()
                 flush.append(out)
+        for _ in range({8: 2, 9: 1, 11: 1}.get(r, 0)):
+            work.pop(0)()
     out = pltpu.make_async_copy(staged[1], vo_hbm, local_sem.at[4])
     out.start()
     flush.append(out)
@@ -517,15 +527,15 @@
 
 
 def handoff(level, t3, t12, lens, q, nk, nv, key_pool, value_pool, out_weight):
-    caps, x_cap = LEVELS[level]
+    caps = LEVELS[level]
     n = len(CHUNKS)
     smem = pl.BlockSpec(memory_space=pltpu.SMEM)
     vmem = pl.BlockSpec(memory_space=pltpu.VMEM)
     hbm = pl.BlockSpec(memory_space=pl.ANY)
     dma = pltpu.SemaphoreType.DMA
     scratch = [pltpu.VMEM((POOL, PAGE, HD), BF)] * 2 + [pltpu.VMEM((2, SPAN, HD), BF)] * 2
-    for pages in (2 * SEND_MINUS, ZROOM, 3 * XFULL, 4 * XFULL):
-        scratch += [pltpu.VMEM((pages, rows, HD), BF) for _, _, rows in CHUNKS]
+    for pages in ((2 * SEND_MINUS,), ZROOM, (3 * XFULL,), (4 * XFULL,)):
+        scratch += [pltpu.VMEM((k, rows, HD), BF) for _, _, rows in CHUNKS for k in pages]
     scratch += [
         pltpu.VMEM((2, 256, SPAN), BF),
         pltpu.VMEM((2, 2, 256, 128), F32),
@@ -538,8 +548,8 @@
         dma((5,)),
         dma((n, 2, 4)),
         dma((n, 2, 4)),
-        dma((n, 3)),
-        dma((n, 3)),
+        dma((n, 2, 3)),
+        dma((n, 2, 3)),
         dma((4,)),
         dma((4,)),
         dma((2, 2, 4)),
@@ -550,7 +560,7 @@
         dma((3,)),
     ]
     return pl.pallas_call(
-        functools.partial(handoff_kernel, caps, x_cap),
+        functools.partial(handoff_kernel, caps),
         out_shape=(
             jax.ShapeDtypeStruct((256, 256), BF),
             jax.ShapeDtypeStruct((2, SPAN, HD), BF),

time: 156 us -> 134 us (0.86)
  Pallas kernels: 149 us -> 126 us
    pallas_call x1, Pallas kernels: 145 us -> 123 us  [handoff(): pl.pallas_call(functools.partial(handoff_kernel, caps), out_shape=(jax.Sh...]
where the time goes in v2:
time: 134 us
  Pallas kernels  126 us (94%)
  local copies, waits for them, and re-layouts  5.77 us (4%)
    pallas_call x1, Pallas kernels, handoff(): pl.pallas_call(functools.partial(handoff_kernel, caps), out_shape=(jax.Sh...  123 us
    unnamed x5, local copies, waits for them, and re-layouts  4.83 us
    pallas_call x1, Pallas kernels, make_tables(): pl.pallas_call(tables_kernel, out_shape=(jax.ShapeDtypeStruct((8, 128), I...  3.49 us

profile of v2, /device:TPU:16, one launch (start us, length us, event | category | flops | bytes accessed | tf_op | source)
XLA Modules:
  0.0 133.7 jit_solution(7471426764946689686)
XLA Ops:
  0.6 3.5 %shard_map.124 = (s32[8,128]{1,0:T(8,128)S(1)}, s32[16,168]{1,0:T(8,128)S(1)}, s32[8,128]{1,0:T(8,128)S(1)}, s32[1]{0:T(128)}) custom-call(s32[64]{0:T(128)} %len_ref.1, s32[64]{0:T(128)} %assign_ref.1, s32[64,80]{1,0:T(8,128)} %bt_ref.1), custom_call_target="tpu_custom_call" | custom-call | tf_op jit(solution)/shard_map/pallas_call | solution.py:189
  4.8 0.9 reshape.18
  5.7 123.2 %conditional.1 = ((bf16[256,256]{1,0:T(8,128)(2,1)S(1)}, bf16[2,5120,128]{2,1,0:T(8,128)(2,1)S(1)}, bf16[2,5120,128]{2,1,0:T(8,128)(2,1)})) conditional(s32[]{:T(128)} %bitcast, (s32[8,128]{1,0:T(8,128)S(1)}, s32[16,168]{1,0:T(8,128)S(1)}, s32[8,128]{1,0:T(8,128)S(1)}, bf16[64,1024]{1,0:T(8,128)(2,1)S(1)}, ...), branch_computations={%region_0.0_spmd, %region_1.0_spmd, %region_2.0_spmd, %region_3.0_... | conditional | bytes 8 | solution.py:584
  5.7 122.6 %branch_0_fun.1 = (bf16[256,256]{1,0:T(8,128)(2,1)S(1)}, bf16[2,5120,128]{2,1,0:T(8,128)(2,1)S(1)}, bf16[2,5120,128]{2,1,0:T(8,128)(2,1)}) custom-call(s32[8,128]{1,0:T(8,128)S(1)} %get-tuple-element.72.refs_0_, s32[16,168]{1,0:T(8,128)S(1)} %get-tuple-element.73.refs_1_, s32[8,128]{1,0:T(8,128)S(1)} %get-tuple-element.74.refs_2_, ...), custom_call_target="tpu_custom_call" | custom-call | tf_op jit(solution)/shard_map/cond/branch_0_fun/pallas_call | solution.py:562
  128.9 0.7 copy.39
  129.6 0.0 copy-start
  129.6 1.5 %copy.40 = bf16[2,5120,128]{2,1,0:T(8,128)(2,1)} copy(bf16[2,5120,128]{2,1,0:T(8,128)(2,1)S(1)} %get-tuple-element.150) | data formatting | bytes 5242880
  131.0 1.2 copy-done
  132.2 1.5 %copy.41 = bf16[2,5120,128]{2,1,0:T(8,128)(2,1)} copy(bf16[2,5120,128]{2,1,0:T(8,128)(2,1)S(1)} %copy-done) | data formatting | bytes 5242880
Async XLA Ops:
  129.6 2.7 %copy-start = (bf16[2,5120,128]{2,1,0:T(8,128)(2,1)S(1)}, bf16[2,5120,128]{2,1,0:T(8,128)(2,1)}, u32[]{:S(2)}) copy-start(bf16[2,5120,128]{2,1,0:T(8,128)(2,1)} %get-tuple-element.151) | copy-start | bytes 7864324
